TPU v7x, 128 devices: a whole 4x4x4 slice. The times are simulated.
128 devices in a mesh: row: 8 (over z, core), col: 16 (over y, x).
Axes of the slice: x: 4, y: 4, z: 4, core: 2. Of those that a mesh axis runs over, the one named last changes fastest.
Arguments:
- operator: float32 [16384, 16384], P('row', 'col'), may hold values from -0.046875 to 0.046875
- vectors: float32 [16384, 256], P('row', 'col'), may hold values from -6 to 6
- owner_map: int32 [11264, 1], P(('row', 'col')), may hold values from 0 to 15; in each aligned block of 88 rows (0 to 87, 88 to 175, ...) at most 16 rows name the same one
- coupling: float32 [8, 512, 1024], P('row', 'col'), may hold values from -0.1875 to 0.1875
- ancestors: int32 [8, 16, 512], P('row', 'col'), may hold values from 0 to 1535, as said below
- leaf_modes: float32 [8, 16, 2048, 256], P('row', 'col'), may hold values from -0.375 to 0.375
- constraint_modes: float32 [8, 16, 2048, 512], P('row', 'col'), may hold values from -0.25 to 0.25
Outputs:
- separators: float32 [8, 512, 256], P('row', 'col')
- interiors: float32 [8, 16, 2048, 256], P('row', 'col')
Inputs may be any that keep to these rules, and one draw needn't show every extreme that they name: `owner_map`: in each aligned block of 88 rows no leaf is named more than 16 times, a bound that some block reaches. `ancestors`: the 512 indices of one leaf are distinct.
All inputs are finite; a program needn't handle non-finite values.
Results may differ from a plain program's by a relative error of at most 0.00007.
Values sent between devices are 32-bit elements; how exact they have to be, the bound alone decides.
A program may use at most 64 MiB of HBM per device.

v0:
```python
import jax
import jax.numpy as jnp
from jax import lax
from jax.sharding import PartitionSpec as P

highest = lax.Precision.HIGHEST


def slot_ranks(owned_rows):
    rows = owned_rows.shape[0]
    place = jnp.arange(rows, dtype=jnp.int32)
    same = (owned_rows[:, None] == owned_rows[None, :]) & (place[None, :] < place[:, None])
    return jnp.sum(same.astype(jnp.int32), axis=1)


def on_device(operator, vectors, owner_map, coupling, ancestors, leaf_modes, constraint_modes):
    fanout = lax.axis_size("col")
    mode_local = owner_map.shape[0]
    separator_local = coupling.shape[1]
    mode_count = leaf_modes.shape[3]
    slot_count = mode_count // fanout
    mode_matrix = leaf_modes[0, 0]
    partial_adjoint = lax.dot_general(
        operator,
        lax.all_gather(vectors, "col", axis=1, tiled=True),
        (((0,), (0,)), ((), ())),
        precision=highest,
        preferred_element_type=jnp.float32,
    )
    adjoint = lax.psum(partial_adjoint, "row")
    forward = jnp.dot(operator, adjoint, precision=highest, preferred_element_type=jnp.float32)
    vector_count = forward.shape[1]
    local_rows = lax.psum_scatter(forward, "col", scatter_dimension=0, tiled=True)
    mode_rows = local_rows[:mode_local]
    separator_raw = local_rows[mode_local : mode_local + separator_local]
    top_local = local_rows[mode_local + separator_local :]
    owned_here = owner_map[:, 0]
    target = owned_here * slot_count + slot_ranks(owned_here)
    source = (
        jnp.full((fanout * slot_count,), mode_local, jnp.int32)
        .at[target]
        .set(jnp.arange(mode_local, dtype=jnp.int32))
    )
    outgoing = jnp.take(mode_rows, source, axis=0, mode="fill", fill_value=0.0).reshape(
        fanout, slot_count, vector_count
    )
    received = lax.all_to_all(outgoing, "col", split_axis=0, concat_axis=0, tiled=True)
    flattened = received.reshape(mode_count, received.shape[2])
    modal_sum = jnp.dot(
        mode_matrix, flattened, precision=highest, preferred_element_type=jnp.float32
    )
    top_gathered = lax.all_gather(top_local, ("row", "col"), axis=0, tiled=True)
    separators = separator_raw + jnp.dot(
        coupling[0], top_gathered, precision=highest, preferred_element_type=jnp.float32
    )
    separator_all = lax.all_gather(separators, "col", axis=0, tiled=True)
    candidates = jnp.concatenate([top_gathered, separator_all], axis=0)
    picked = jnp.take(candidates, ancestors[0, 0], axis=0)
    interiors = modal_sum + jnp.dot(
        constraint_modes[0, 0], picked, precision=highest, preferred_element_type=jnp.float32
    )
    return (separators[None], interiors[None, None])


def solution(mesh):
    in_specs = (
        P("row", "col"),
        P("row", "col"),
        P(("row", "col"), None),
        P("row", "col", None),
        P("row", "col", None),
        P("row", "col", None, None),
        P("row", "col", None, None),
    )
    out_specs = (P("row", "col", None), P("row", "col", None, None))
    return jax.shard_map(
        on_device, mesh=mesh, in_specs=in_specs, out_specs=out_specs, check_vma=False
    )
```

profile of v0, /device:TPU:0, one launch (start us, length us, event | category | flops | bytes accessed | tf_op | source)
XLA Modules:
  0.0 350.4 jit_solution(16381814410100779000)
XLA Ops:
  7.2 0.7 all-gather.3.cloned.1.call-update
  8.0 49.5 %all-gather.3.cloned.1.call-done = f32[2048,256]{0,1:T(8,128)} async-done(((f32[2048,16]{0,1:T(8,128)}), f32[2048,256]{0,1:T(8,128)}) %all-gather.3.cloned.1.call-update) | async-done | bytes 2097168 | tf_op jit(solution)/shard_map/all_gather | solution.py:25
  57.4 17.0 %fusion.14 = f32[1024,256]{1,0:T(8,128)} fusion(f32[2048,1024]{1,0:T(8,128)} %param.7, f32[2048,256]{0,1:T(8,128)} %all-gather.3.cloned.1.call-done), kind=kOutput, calls=%fused_computation.33 | convolution fusion | flops 6442450944 | bytes 11534336 | tf_op jit(solution)/shard_map/dot_general | solution.py:23
  74.5 0.2 reduce-scatter.2.cloned.1.call-start
  74.7 62.0 %all-reduce.2.cloned.1.call-done = f32[1024,256]{1,0:T(8,128)} async-done(((f32[1024,256]{1,0:T(8,128)}), f32[1024,256]{1,0:T(8,128)}) %all-reduce.2.cloned.1.call-update) | async-done | bytes 1048592 | tf_op jit(solution)/shard_map/psum | solution.py:30
  136.7 17.1 %convolution_bitcast_fusion = f32[2048,256]{0,1:T(8,128)} fusion(f32[1024,256]{1,0:T(8,128)} %all-reduce.2.cloned.1.call-done, f32[2048,1024]{1,0:T(8,128)} %param.7), kind=kOutput, calls=%fused_computation.7 | convolution fusion | flops 6442450944 | bytes 11534336 | tf_op jit(solution)/shard_map/dot_general | solution.py:31
  153.8 73.4 %reduce-scatter.2.cloned.1.call-done = f32[128,256]{0,1:T(8,128)} async-done(((f32[2048,256]{0,1:T(8,128)}), f32[128,256]{0,1:T(8,128)}) %reduce-scatter.2.cloned.1.call-update) | async-done | bytes 131088 | tf_op jit(solution)/shard_map/reduce_scatter | solution.py:33
  227.3 1.1 slice.17
  228.3 0.7 copy.25
  229.0 0.2 convert_reduce_fusion
  229.2 0.8 scatter_custom_fusion
  230.2 1.0 copy.27
  231.2 1.0 gather_fusion
  232.2 0.8 broadcast_select_fusion
  233.0 4.9 %all-to-all-start = ((f32[16,16,256]{2,1,0:T(8,128)}), f32[16,16,256]{2,1,0:T(8,128)}, u32[]{:S(2)}, u32[]{:S(2)}) async-start(f32[16,16,256]{2,1,0:T(8,128)} %broadcast_select_fusion), calls=%async_computation.1 | async-start | bytes 524288 | tf_op jit(solution)/shard_map/all_to_all | solution.py:47
  237.9 55.8 %all-gather.5.cloned.1.call-done = f32[1024,256]{1,0:T(8,128)} async-done(((f32[8,256]{1,0:T(8,128)}), f32[1024,256]{1,0:T(8,128)}) %all-gather.5.cloned.1.call-update) | async-done | bytes 1048592 | tf_op jit(solution)/shard_map/all_gather | solution.py:52
  293.7 3.1 fusion.4
  296.9 0.7 copy.29
  297.6 22.3 %all_gather.11 = f32[512,256]{1,0:T(8,128)S(1)} all-gather(f32[32,256]{1,0:T(8,128)S(1)} %copy.28), channel_id=1, replica_groups=mesh['row'=8,'col'=16] {'col'}, dimensions={0}, use_global_device_ids=true | all-gather | bytes 557056 | tf_op jit(solution)/shard_map/all_gather | solution.py:56
  319.9 1.2 pad_maximum_fusion
  321.1 3.0 gather_fusion.1
  324.1 10.4 %fusion = f32[256,2048]{1,0:T(8,128)} fusion(f32[1,1,2048,512]{3,2,1,0:T(8,128)} %param.13, f32[512,256]{1,0:T(8,128)S(1)} %gather_fusion.1, pred[512]{0:T(512)(128)(4,1)S(1)} %compare_and_fusion), kind=kOutput, calls=%fused_computation.3 | convolution fusion | flops 3221356544 | bytes 6816256 | tf_op jit(solution)/shard_map/dot_general | solution.py:59
  334.5 6.5 %fusion.2 = f32[1,1,2048,256]{2,3,1,0:T(8,128)} fusion(f32[256,2048]{1,0:T(8,128)} %fusion, f32[256,256]{1,0:T(8,128)} %bitcast.8, f32[1,1,2048,256]{3,2,1,0:T(8,128)S(1)} %copy-done), kind=kOutput, calls=%fused_computation.6 | convolution fusion | flops 1611137024 | bytes 6553600 | tf_op jit(solution)/shard_map/dot_general | solution.py:49
  341.0 2.9 copy.30
  (29 shorter events, 0.4 us)
Async XLA Ops:
  7.2 327.3 %copy-start = (f32[1,1,2048,256]{3,2,1,0:T(8,128)S(1)}, f32[1,1,2048,256]{3,2,1,0:T(8,128)}, u32[]{:S(2)}) copy-start(f32[1,1,2048,256]{3,2,1,0:T(8,128)} %param.12) | copy-start | bytes 6291460
  7.2 50.3 %all-gather.3.cloned.1.call-start = ((), (), s32[]{:S(2)}) async-start(), calls=%async_computation.2 | async-start | bytes 2228224 | tf_op jit(solution)/shard_map/all_gather | solution.py:25
  7.9 128.8 %all-reduce.2.cloned.1.call-start = ((), (), s32[]{:S(2)}) async-start(), calls=%async_computation.3 | async-start | bytes 2097152 | tf_op jit(solution)/shard_map/psum | solution.py:30
  74.5 152.8 %reduce-scatter.2.cloned.1.call-start = ((), (), s32[]{:S(2)}) async-start(), calls=%async_computation.4 | async-start | bytes 2228224 | tf_op jit(solution)/shard_map/reduce_scatter | solution.py:33
  153.7 75.3 %copy-start.5 = (s32[88,1]{0,1:T(1,128)S(1)}, s32[88,1]{0,1:T(1,128)}, u32[]{:S(2)}) copy-start(s32[88,1]{0,1:T(1,128)} %param.9) | copy-start | bytes 1060
  153.8 76.4 %copy-start.4 = (s32[1,1,512]{2,1,0:T(1,128)S(1)}, s32[1,1,512]{2,1,0:T(1,128)}, u32[]{:S(2)}) copy-start(s32[1,1,512]{2,1,0:T(1,128)} %param.11) | copy-start | bytes 6148
  153.8 140.0 %copy-start.3 = (f32[1,32,1024]{2,1,0:T(8,128)S(1)}, f32[1,32,1024]{2,1,0:T(8,128)}, u32[]{:S(2)}) copy-start(f32[1,32,1024]{2,1,0:T(8,128)} %param.10) | copy-start | bytes 393220
  153.8 140.0 %all-gather.5.cloned.1.call-start = ((), (), s32[]{:S(2)}) async-start(), calls=%async_computation.5 | async-start | bytes 1056768 | tf_op jit(solution)/shard_map/all_gather | solution.py:52
  227.2 66.5 %copy-start.2 = (f32[128,256]{0,1:T(8,128)S(1)}, f32[128,256]{0,1:T(8,128)}, u32[]{:S(2)}) copy-start(f32[128,256]{0,1:T(8,128)} %reduce-scatter.2.cloned.1.call-done) | copy-start | bytes 393220
  233.0 101.5 %all-to-all-start = ((f32[16,16,256]{2,1,0:T(8,128)}), f32[16,16,256]{2,1,0:T(8,128)}, u32[]{:S(2)}, u32[]{:S(2)}) async-start(f32[16,16,256]{2,1,0:T(8,128)} %broadcast_select_fusion), calls=%async_computation.1 | async-start | bytes 524288 | tf_op jit(solution)/shard_map/all_to_all | solution.py:47
  293.7 26.1 %copy-start.1 = (f32[1024,256]{1,0:T(8,128)S(1)}, f32[1024,256]{1,0:T(8,128)}, u32[]{:S(2)}) copy-start(f32[1024,256]{1,0:T(8,128)} %all-gather.5.cloned.1.call-done) | copy-start | bytes 3145732
Sparse Core Ops, SparseCore 0:
  10.2 47.2 all-gather.2
  74.6 62.0 all-reduce.1
  153.9 73.3 reduce-scatter.1
  230.8 62.8 all-gather.4
where the time goes:
time: 351 us; the launch traced here: 350 us
  waiting for transfers between devices  241 us (69%)
  matrix products  54.1 us (15%)
  blocking collectives  22.3 us (6%)
  between operations  13.9 us (4%)
  local copies, waits for them, and re-layouts  11.3 us (3%)
  starting transfers between devices  5.23 us (1%)
    reduce_scatter x1, waiting for transfers between devices, on_device(): lax.psum_scatter(forward, 'col', scatter_dimension=0, tiled=True)  73.4 us
    psum x1, waiting for transfers between devices, on_device(): adjoint = lax.psum(partial_adjoint, 'row')  62 us
    all_gather x1, waiting for transfers between devices, on_device(): top_gathered = lax.all_gather(top_local, ('row', 'col'), axis=0, tiled=True)  55.8 us
    all_gather x1, waiting for transfers between devices, on_device(): lax.all_gather(vectors, 'col', axis=1, tiled=True)  49.5 us
    all_gather x1, blocking collectives, on_device(): separator_all = lax.all_gather(separators, 'col', axis=0, tiled=True)  22.3 us
    dot_general x1, matrix products, on_device(): jnp.dot(operator, adjoint, precision=highest, preferred_element_type=jnp....  17.1 us
    dot_general x1, matrix products, on_device(): lax.dot_general(operator, lax.all_gather(vectors, 'col', axis=1, tiled=Tr...  17 us
    dot_general x1, matrix products, on_device(): jnp.dot(constraint_modes[0, 0], picked, precision=highest, preferred_elem...  10.4 us
  transfers between devices with their start and end apart: 5, of which 4 were waited for; matrix products, arithmetic and copies ran while one was open for 6% of the time, Pallas kernels for 0%

commit v1 on v0

--- a/solution.py
+++ b/solution.py
@@ -4,6 +4,12 @@
 from jax.sharding import PartitionSpec as P
 
 highest = lax.Precision.HIGHEST
+
+
+def gather_by_exchange(x, axis, dim):
+    size = lax.axis_size(axis)
+    repeats = [size if d == dim else 1 for d in range(x.ndim)]
+    return lax.all_to_all(jnp.tile(x, repeats), axis, split_axis=dim, concat_axis=dim, tiled=True)
 
 
 def slot_ranks(owned_rows):
@@ -22,7 +28,7 @@
     mode_matrix = leaf_modes[0, 0]
     partial_adjoint = lax.dot_general(
         operator,
-        lax.all_gather(vectors, "col", axis=1, tiled=True),
+        gather_by_exchange(vectors, "col", 1),
         (((0,), (0,)), ((), ())),
         precision=highest,
         preferred_element_type=jnp.float32,

time: 351 us -> 336 us (0.957)
  waiting for transfers between devices: 241 us -> 191 us
  blocking collectives: 22.3 us -> 57.6 us
    all_gather x1 -> x0, waiting for transfers between devices: 49.5 us -> none  [on_device(): lax.all_gather(vectors, 'col', axis=1, tiled=True)]
    all_to_all x0 -> x1, blocking collectives: none -> 35.3 us  [gather_by_exchange(): lax.all_to_all(jnp.tile(x, repeats), axis, split_axis=dim, concat_axis=di...]
  transfers between devices with their start and end apart: 5 -> 4, of which waited for: 4 -> 3; matrix products, arithmetic and copies ran while one was open for 6% -> 7% of each run, Pallas kernels for 0% -> 0%
where the time goes in v1:
time: 336 us; the launch traced here: 335 us
  waiting for transfers between devices  191 us (57%)
  blocking collectives  57.6 us (17%)
  matrix products  53.4 us (16%)
  between operations  13.9 us (4%)
  local copies, waits for them, and re-layouts  12.6 us (4%)
  starting transfers between devices  5.2 us (2%)
    reduce_scatter x1, waiting for transfers between devices, on_device(): lax.psum_scatter(forward, 'col', scatter_dimension=0, tiled=True)  73.4 us
    psum x1, waiting for transfers between devices, on_device(): adjoint = lax.psum(partial_adjoint, 'row')  61.1 us
    all_gather x1, waiting for transfers between devices, on_device(): top_gathered = lax.all_gather(top_local, ('row', 'col'), axis=0, tiled=True)  55.9 us
    all_to_all x1, blocking collectives, gather_by_exchange(): lax.all_to_all(jnp.tile(x, repeats), axis, split_axis=dim, concat_axis=di...  35.3 us
    all_gather x1, blocking collectives, on_device(): separator_all = lax.all_gather(separators, 'col', axis=0, tiled=True)  22.3 us
    dot_general x1, matrix products, on_device(): jnp.dot(operator, adjoint, precision=highest, preferred_element_type=jnp....  17.1 us
    dot_general x1, matrix products, on_device(): lax.dot_general(operator, gather_by_exchange(vectors, 'col', 1), (((0,),...  16.3 us
    dot_general x1, matrix products, on_device(): jnp.dot(constraint_modes[0, 0], picked, precision=highest, preferred_elem...  10.4 us
  transfers between devices with their start and end apart: 4, of which 3 were waited for; matrix products, arithmetic and copies ran while one was open for 7% of the time, Pallas kernels for 0%

profile of v1, /device:TPU:0, one launch (start us, length us, event | category | flops | bytes accessed | tf_op | source)
XLA Modules:
  0.0 335.4 jit_solution(14078871965175261668)
XLA Ops:
  7.2 1.3 tile.2
  8.5 35.3 %all_to_all.14 = f32[2048,16,16]{0,2,1:T(8,128)S(1)} all-to-all(f32[2048,16,16]{0,2,1:T(8,128)S(1)} %tile.2), channel_id=1, replica_groups=mesh['row'=8,'col'=16] {'col'}, dimensions={1} | all-to-all | bytes 4194304 | tf_op jit(solution)/shard_map/all_to_all | solution.py:12
  43.8 16.3 %fusion.14 = f32[1024,256]{1,0:T(8,128)} fusion(f32[2048,1024]{1,0:T(8,128)} %param.7, f32[2048,256]{0,1:T(8,128)S(1)} %bitcast.42), kind=kOutput, calls=%fused_computation.33 | convolution fusion | flops 6442450944 | bytes 11534336 | tf_op jit(solution)/shard_map/dot_general | solution.py:29
  60.1 0.2 reduce-scatter.2.cloned.1.call-start
  60.4 61.1 %all-reduce.2.cloned.1.call-done = f32[1024,256]{1,0:T(8,128)} async-done(((f32[1024,256]{1,0:T(8,128)}), f32[1024,256]{1,0:T(8,128)}) %all-reduce.2.cloned.1.call-update) | async-done | bytes 1048592 | tf_op jit(solution)/shard_map/psum | solution.py:36
  121.5 17.1 %convolution_bitcast_fusion = f32[2048,256]{0,1:T(8,128)} fusion(f32[1024,256]{1,0:T(8,128)} %all-reduce.2.cloned.1.call-done, f32[2048,1024]{1,0:T(8,128)} %param.7), kind=kOutput, calls=%fused_computation.7 | convolution fusion | flops 6442450944 | bytes 11534336 | tf_op jit(solution)/shard_map/dot_general | solution.py:37
  138.7 73.4 %reduce-scatter.2.cloned.1.call-done = f32[128,256]{0,1:T(8,128)} async-done(((f32[2048,256]{0,1:T(8,128)}), f32[128,256]{0,1:T(8,128)}) %reduce-scatter.2.cloned.1.call-update) | async-done | bytes 131088 | tf_op jit(solution)/shard_map/reduce_scatter | solution.py:39
  212.1 1.1 slice.17
  213.1 0.7 copy.26
  213.8 0.2 convert_reduce_fusion
  214.0 0.8 scatter_custom_fusion
  215.1 1.0 copy.28
  216.1 1.0 gather_fusion
  217.0 0.8 broadcast_select_fusion
  217.8 4.9 %all-to-all-start.1 = ((f32[16,16,256]{2,1,0:T(8,128)}), f32[16,16,256]{2,1,0:T(8,128)}, u32[]{:S(2)}, u32[]{:S(2)}) async-start(f32[16,16,256]{2,1,0:T(8,128)} %broadcast_select_fusion), calls=%async_computation.2 | async-start | bytes 524288 | tf_op jit(solution)/shard_map/all_to_all | solution.py:53
  222.8 55.9 %all-gather.2.cloned.1.call-done = f32[1024,256]{1,0:T(8,128)} async-done(((f32[8,256]{1,0:T(8,128)}), f32[1024,256]{1,0:T(8,128)}) %all-gather.2.cloned.1.call-update) | async-done | bytes 1048592 | tf_op jit(solution)/shard_map/all_gather | solution.py:58
  278.7 3.1 fusion.4
  281.9 0.7 copy.30
  282.6 22.3 %all_gather.7 = f32[512,256]{1,0:T(8,128)S(1)} all-gather(f32[32,256]{1,0:T(8,128)S(1)} %copy.29), channel_id=1, replica_groups=mesh['row'=8,'col'=16] {'col'}, dimensions={0}, use_global_device_ids=true | all-gather | bytes 557056 | tf_op jit(solution)/shard_map/all_gather | solution.py:62
  304.8 1.2 pad_maximum_fusion
  306.1 3.0 gather_fusion.1
  309.1 10.4 %fusion = f32[256,2048]{1,0:T(8,128)} fusion(f32[1,1,2048,512]{3,2,1,0:T(8,128)} %param.13, f32[512,256]{1,0:T(8,128)S(1)} %gather_fusion.1, pred[512]{0:T(512)(128)(4,1)S(1)} %compare_and_fusion), kind=kOutput, calls=%fused_computation.3 | convolution fusion | flops 3221356544 | bytes 6816256 | tf_op jit(solution)/shard_map/dot_general | solution.py:65
  319.4 6.5 %fusion.2 = f32[1,1,2048,256]{2,3,1,0:T(8,128)} fusion(f32[256,2048]{1,0:T(8,128)} %fusion, f32[256,256]{1,0:T(8,128)} %bitcast.9, f32[1,1,2048,256]{3,2,1,0:T(8,128)S(1)} %copy-done), kind=kOutput, calls=%fused_computation.6 | convolution fusion | flops 1611137024 | bytes 6553600 | tf_op jit(solution)/shard_map/dot_general | solution.py:55
  326.0 2.9 copy.31
  (28 shorter events, 0.4 us)
Async XLA Ops:
  7.2 312.3 %copy-start = (f32[1,1,2048,256]{3,2,1,0:T(8,128)S(1)}, f32[1,1,2048,256]{3,2,1,0:T(8,128)}, u32[]{:S(2)}) copy-start(f32[1,1,2048,256]{3,2,1,0:T(8,128)} %param.12) | copy-start | bytes 6291460
  7.2 114.3 %all-reduce.2.cloned.1.call-start = ((), (), s32[]{:S(2)}) async-start(), calls=%async_computation.3 | async-start | bytes 2097152 | tf_op jit(solution)/shard_map/psum | solution.py:36
  60.1 151.9 %reduce-scatter.2.cloned.1.call-start = ((), (), s32[]{:S(2)}) async-start(), calls=%async_computation.4 | async-start | bytes 2228224 | tf_op jit(solution)/shard_map/reduce_scatter | solution.py:39
  138.6 75.3 %copy-start.5 = (s32[88,1]{0,1:T(1,128)S(1)}, s32[88,1]{0,1:T(1,128)}, u32[]{:S(2)}) copy-start(s32[88,1]{0,1:T(1,128)} %param.9) | copy-start | bytes 1060
  138.6 76.4 %copy-start.4 = (s32[1,1,512]{2,1,0:T(1,128)S(1)}, s32[1,1,512]{2,1,0:T(1,128)}, u32[]{:S(2)}) copy-start(s32[1,1,512]{2,1,0:T(1,128)} %param.11) | copy-start | bytes 6148
  138.6 140.1 %copy-start.3 = (f32[1,32,1024]{2,1,0:T(8,128)S(1)}, f32[1,32,1024]{2,1,0:T(8,128)}, u32[]{:S(2)}) copy-start(f32[1,32,1024]{2,1,0:T(8,128)} %param.10) | copy-start | bytes 393220
  138.6 140.1 %all-gather.2.cloned.1.call-start = ((), (), s32[]{:S(2)}) async-start(), calls=%async_computation.5 | async-start | bytes 1056768 | tf_op jit(solution)/shard_map/all_gather | solution.py:58
  212.1 66.6 %copy-start.2 = (f32[128,256]{0,1:T(8,128)S(1)}, f32[128,256]{0,1:T(8,128)}, u32[]{:S(2)}) copy-start(f32[128,256]{0,1:T(8,128)} %reduce-scatter.2.cloned.1.call-done) | copy-start | bytes 393220
  217.8 101.6 %all-to-all-start.1 = ((f32[16,16,256]{2,1,0:T(8,128)}), f32[16,16,256]{2,1,0:T(8,128)}, u32[]{:S(2)}, u32[]{:S(2)}) async-start(f32[16,16,256]{2,1,0:T(8,128)} %broadcast_select_fusion), calls=%async_computation.2 | async-start | bytes 524288 | tf_op jit(solution)/shard_map/all_to_all | solution.py:53
  278.7 26.1 %copy-start.1 = (f32[1024,256]{1,0:T(8,128)S(1)}, f32[1024,256]{1,0:T(8,128)}, u32[]{:S(2)}) copy-start(f32[1024,256]{1,0:T(8,128)} %all-gather.2.cloned.1.call-done) | copy-start | bytes 3145732
Sparse Core Ops, SparseCore 0:
  60.3 61.1 all-reduce.1
  138.7 73.3 reduce-scatter.1
  215.8 62.8 all-gather.1
